TPU v7x, 32 devices: a whole 2x2x4 slice. The times are simulated.
32 devices in a mesh: row: 8 (over y, x, core), col: 4 (over z).
Axes of the slice: x: 2, y: 2, z: 4, core: 2. Of those that a mesh axis runs over, the one named last changes fastest.
Arguments:
- diag_tile: float32 [256, 256], replicated, may hold values from 0 to 10, as said below
- panel_block: float32 [12288, 256], P(('row', 'col')), may hold values from -3 to 3
- trailing: bfloat16 [12288, 12288], P('row', 'col'), may hold values from -6 to 6
- vec_head: float32 [512, 256], P('col'), may hold values from -6 to 6
- vec_rest: float32 [512, 12288], P('col', 'row'), may hold values from -6 to 6
Outputs:
- panel: float32 [12288, 256], P(('row', 'col'))
- trailing_new: bfloat16 [12288, 12288], P('row', 'col')
- whitened: float32 [512, 256], P('col')
- vec_new: float32 [512, 12288], P('col', 'row')
Inputs may be any that keep to these rules, and one draw needn't show every extreme that they name: `diag_tile`: symmetric positive definite.
All inputs are finite; a program needn't handle non-finite values.
Results may differ from a plain program's by a relative error of at most 0.0054.
Values may be sent and summed in bfloat16 or wider, within the bound.
No kernel may reach another device: no remote copies, remote signals or barrier semaphores. Data moves between devices by JAX's collectives and lax.ppermute only.
A program may use at most 128 MiB of HBM per device.

v0:
```python
import jax
import jax.numpy as jnp
from jax import lax
from jax.sharding import PartitionSpec as P


def right_solve(factor, rhs):
    return lax.linalg.triangular_solve(factor, rhs, left_side=False, lower=True, transpose_a=True)


def per_device(diag_tile, panel_block, trailing, vec_head, vec_rest):
    factor = jnp.linalg.cholesky(diag_tile)
    panel = right_solve(factor, panel_block)
    panel_half = panel.astype(jnp.bfloat16)
    row_panel = lax.all_gather(panel_half, "col", axis=0, tiled=True)
    complete = lax.all_gather(row_panel, "row", axis=0, tiled=True)
    width = trailing.shape[1]
    col_panel = lax.dynamic_slice_in_dim(complete, lax.axis_index("col") * width, width, 0)
    update = lax.dot_general(
        row_panel, col_panel, (((1,), (1,)), ((), ())), preferred_element_type=jnp.float32
    )
    trailing_new = (trailing.astype(jnp.float32) - update).astype(jnp.bfloat16)
    whitened = right_solve(factor, vec_head)
    whitened_half = whitened.astype(jnp.bfloat16)
    product = lax.dot_general(
        whitened_half, row_panel, (((1,), (1,)), ((), ())), preferred_element_type=jnp.float32
    )
    vec_new = vec_rest - product
    return (panel, trailing_new, whitened, vec_new)


def solution(mesh):
    in_specs = (P(), P(("row", "col"), None), P("row", "col"), P("col", None), P("col", "row"))
    out_specs = (P(("row", "col"), None), P("row", "col"), P("col", None), P("col", "row"))
    return jax.shard_map(
        per_device, mesh=mesh, in_specs=in_specs, out_specs=out_specs, check_vma=False
    )
```

profile of v0, /device:TPU:0, one launch (start us, length us, event | category | flops | bytes accessed | tf_op | source)
XLA Modules:
  0.0 157.3 jit_solution(15783590068085898557)
XLA Ops:
  7.2 0.0 copy-start.1
  7.2 0.0 copy-start
  7.2 0.0 all-gather.2.cloned.1.call-start
  7.2 1.1 copy.9
  8.4 1.0 fusion.1
  9.4 11.7 %cholesky.50 = f32[128,128]{1,0:T(8,128)S(1)} custom-call(f32[128,128]{1,0:T(8,128)S(1)} %cholesky.118), custom_call_target="Cholesky" | custom-call | tf_op jit(solution)/shard_map/jit(cholesky)/cholesky | solution.py:12
  21.2 9.8 %custom-call.16 = f32[1,128,128]{1,2,0:T(8,128)S(1)} custom-call(f32[1,128,128]{2,1,0:T(8,128)S(1)} %get-tuple-element.29), custom_call_target="InvertDiagBlocksLowerTriangular" | custom-call | tf_op jit(solution)/shard_map/jit(cholesky)/cholesky | solution.py:12
  31.0 0.2 constant_dynamic-update-slice_fusion
  31.2 0.3 convolution_subtract_fusion.3
  31.5 11.7 %cholesky.105 = f32[128,128]{1,0:T(8,128)S(1)} custom-call(f32[128,128]{1,0:T(8,128)S(1)} %convolution_subtract_fusion.3), custom_call_target="Cholesky" | custom-call | tf_op jit(solution)/shard_map/jit(cholesky)/cholesky | solution.py:12
  43.2 0.6 compare_reduce_fusion
  45.2 0.1 triangular_solve.76
  45.3 4.1 %while.1 = (s32[]{:T(128)}, f32[256,256]{1,0:T(8,128)S(1)}, s32[2,2]{1,0:T(2,128)S(1)}, f32[2,128,128]{2,1,0:T(8,128)S(1)}, s32[]{:T(128)}) while((s32[]{:T(128)}, f32[256,256]{1,0:T(8,128)S(1)}, s32[2,2]{1,0:T(2,128)S(1)}, f32[2,128,128]{2,1,0:T(8,128)S(1)}, s32[]{:T(128)}) %tuple.28), condition=%wide.while_cond, body=%wide.while_body.sunk | while | flops 2 | bytes 131189 | solution.py:8
  45.4 0.6 fusion.26
  46.0 1.4 bitcast_dynamic-update-slice_fusion.2
  47.4 0.6 fusion.26
  48.0 1.4 bitcast_dynamic-update-slice_fusion.2
  49.4 19.7 %custom-call.17 = f32[2,128,128]{1,2,0:T(8,128)S(1)} custom-call(f32[2,128,128]{2,1,0:T(8,128)S(1)} %get-tuple-element.11), custom_call_target="InvertDiagBlocksLowerTriangular" | custom-call | tf_op jit(solution)/shard_map/triangular_solve | solution.py:8
  69.1 1.3 fusion.2
  70.4 1.4 convolution_subtract_fusion.1
  71.9 0.4 fusion.11
  72.3 21.8 %all_gather.6 = bf16[1536,256]{0,1:T(8,128)(2,1)} all-gather(bf16[384,256]{0,1:T(8,128)(2,1)S(1)} %fusion.15), channel_id=1, replica_groups=mesh['row'=8,'col'=4] {'col'}, dimensions={0}, use_global_device_ids=true | all-gather | bytes 983040 | tf_op jit(solution)/shard_map/all_gather | solution.py:15
  94.1 0.0 all-gather.2.cloned.1.call-update
  94.2 0.9 copy.10
  95.1 0.0 copy-done.1
  95.1 0.3 fusion.8
  95.4 0.3 convolution_subtract_fusion.2
  95.7 0.3 fusion.10
  96.0 0.8 copy.11
  96.7 2.3 %convolution_subtract_fusion = f32[128,1536]{1,0:T(8,128)} fusion(f32[128,1536]{1,0:T(8,128)S(1)} %copy-done, bf16[1536,256]{0,1:T(8,128)(2,1)} %all_gather.6, f32[128,128]{0,1:T(8,128)S(1)} %fusion.10, f32[128,128]{0,1:T(8,128)S(1)} %bitcast.42), kind=kOutput, calls=%fused_computation.3 | convolution fusion | flops 100990976 | bytes 2490368 | tf_op jit(solution)/shard_map/dot_general | solution.py:25
  99.1 40.6 %all-gather.2.cloned.1.call-done = bf16[12288,256]{0,1:T(8,128)(2,1)} async-done(((bf16[1536,256]{0,1:T(8,128)(2,1)}), bf16[12288,256]{0,1:T(8,128)(2,1)}) %all-gather.2.cloned.1.call-update) | async-done | bytes 6291472 | tf_op jit(solution)/shard_map/all_gather | solution.py:16
  139.6 10.8 %subtract_convert_fusion = bf16[1536,3072]{1,0:T(8,128)(2,1)} fusion(bf16[1536,3072]{1,0:T(8,128)(2,1)} %param.7, bf16[1536,256]{0,1:T(8,128)(2,1)} %all_gather.6, bf16[12288,256]{0,1:T(8,128)(2,1)} %all-gather.2.cloned.1.call-done, s32[]{:T(128)S(6)} %select_n.8), kind=kOutput, calls=%fused_computation.2 | convolution fusion | flops 2430074880 | bytes 21233668 | tf_op jit(solution)/shard_map/dot_general | solution.py:19
  (13 shorter events, 0.2 us)
Async XLA Ops:
  7.2 87.9 %copy-start.1 = (f32[128,256]{1,0:T(8,128)S(1)}, f32[128,256]{1,0:T(8,128)}, u32[]{:S(2)}) copy-start(f32[128,256]{1,0:T(8,128)} %param.8) | copy-start | bytes 393220
  7.2 89.6 %copy-start = (f32[128,1536]{1,0:T(8,128)S(1)}, f32[128,1536]{1,0:T(8,128)}, u32[]{:S(2)}) copy-start(f32[128,1536]{1,0:T(8,128)} %param.9) | copy-start | bytes 2359300
  7.2 132.5 %all-gather.2.cloned.1.call-start = ((), (), s32[]{:S(2)}) async-start(), calls=%async_computation | async-start | bytes 7077888 | tf_op jit(solution)/shard_map/all_gather | solution.py:16
Sparse Core Ops, SparseCore 0:
  94.3 45.3 all-gather.1
where the time goes:
time: 158 us; the launch traced here: 157 us
  other arithmetic  54.7 us (35%)
  waiting for transfers between devices  40.6 us (26%)
  blocking collectives  21.8 us (14%)
  matrix products  17.6 us (11%)
  between operations  15.5 us (10%)
  local copies, waits for them, and re-layouts  6.87 us (4%)
    all_gather x1, waiting for transfers between devices, per_device(): complete = lax.all_gather(row_panel, 'row', axis=0, tiled=True)  40.6 us
    another operation x6, other arithmetic, per_device(): factor = jnp.linalg.cholesky(diag_tile)  33.9 us
    all_gather x1, blocking collectives, per_device(): row_panel = lax.all_gather(panel_half, 'col', axis=0, tiled=True)  21.8 us
    another operation x5, other arithmetic, right_solve(): lax.linalg.triangular_solve(factor, rhs, left_side=False, lower=True, tra...  19.7 us
    dot_general x1, matrix products, per_device(): lax.dot_general(row_panel, col_panel, (((1,), (1,)), ((), ())), preferred...  10.8 us
    another operation x6, matrix products, right_solve(): lax.linalg.triangular_solve(factor, rhs, left_side=False, lower=True, tra...  4 us
    another operation x6, local copies, waits for them, and re-layouts  3.95 us
  transfers between devices with their start and end apart: 1, of which 1 were waited for; matrix products, arithmetic and copies ran while one was open for 3% of the time, Pallas kernels for 0%

commit v1 on v0

v1 whole, which is shorter than its diff:
```python
import functools

import jax
import jax.numpy as jnp
from jax import lax
from jax.experimental import pallas as pl
from jax.experimental.pallas import tpu as pltpu
from jax.sharding import PartitionSpec as P

LANES = 128
SUB = 8
GROUP = 64
EXACT = lax.Precision.HIGHEST


def eliminate(x, first, last):
    n = x.shape[0]
    halves = n // LANES
    sub = lax.broadcasted_iota(jnp.int32, (SUB, LANES), 0)
    lane = lax.broadcasted_iota(jnp.int32, (SUB, LANES), 1)
    count = GROUP // SUB

    def row_of(value, j):
        return jnp.take_along_axis(value, jnp.full((SUB, LANES), j, jnp.int32), axis=0)

    def col_of(value, l):
        return jnp.broadcast_to(value[:, l : l + 1], (SUB, LANES))

    for r0 in range(first, last, GROUP):
        rows = [
            [x[r0 + SUB * g : r0 + SUB * (g + 1), h * LANES : (h + 1) * LANES] for h in range(halves)]
            for g in range(count)
        ]
        ahead = None
        for b in range(count):
            q = r0 + SUB * b
            hq, lq = q // LANES, q % LANES
            cols = {}
            for j in range(SUB):
                cols[b, j] = col_of(rows[b][hq], lq + j) if ahead is None else ahead[j]
            ahead = None
            if b + 1 < count:
                h1, l1 = (q + SUB) // LANES, (q + SUB) % LANES
                for j in range(SUB):
                    cols[b + 1, j] = col_of(rows[b + 1][hq], lq + j)
                ahead = [col_of(rows[b + 1][h1], l1 + j) for j in range(SUB)]
            for g in range(b + 2, count):
                for j in range(SUB):
                    cols[g, j] = col_of(rows[g][hq], lq + j)
            block = (lane >= lq) & (lane < lq + SUB)
            for g in range(b, count):
                rows[g][hq] = jnp.where(block, 0.0, rows[g][hq])
            rows[b][hq] = jnp.where(lane == lq + sub, 1.0, rows[b][hq])
            pivots = None
            for j in range(SUB):
                pivot = row_of(cols[b, j], j)
                inverse = 1.0 / pivot
                pivots = pivot if pivots is None else jnp.where(sub == j, pivot, pivots)
                across = {l: row_of(cols[b, l], j) for l in range(j + 1, SUB)}
                pivot_row = [row_of(rows[b][h], j) for h in range(halves)]
                if ahead is not None:
                    next_row = [row_of(cols[b + 1, j], l) for l in range(SUB)]
                for g in range(b, count):
                    factor = cols[g, j] * inverse
                    if g == b:
                        if j == SUB - 1:
                            continue
                        factor = jnp.where(sub > j, factor, 0.0)
                    for l in range(j + 1, SUB):
                        cols[g, l] = cols[g, l] - factor * across[l]
                    if g == b + 1:
                        for l in range(SUB):
                            ahead[l] = ahead[l] - factor * next_row[l]
                    for h in range(halves):
                        rows[g][h] = rows[g][h] - factor * pivot_row[h]
            scale = lax.rsqrt(pivots)
            for h in range(halves):
                rows[b][h] = rows[b][h] * scale
        for g in range(count):
            for h in range(halves):
                x[r0 + SUB * g : r0 + SUB * (g + 1), h * LANES : (h + 1) * LANES] = rows[g][h]
        r1 = r0 + GROUP
        done = x[r0:r1, :]
        row_at = lax.broadcasted_iota(jnp.int32, (GROUP, n), 0) + r0
        col_at = lax.broadcasted_iota(jnp.int32, (GROUP, n), 1)
        clean = jnp.where((col_at > row_at) & (col_at < r1), 0.0, done)
        for top, bottom in ((r1, min(r1 + GROUP, n)), (min(r1 + GROUP, n), n)):
            if top < bottom:
                update = lax.dot_general(
                    done[:, top:bottom],
                    clean,
                    (((0,), (0,)), ((), ())),
                    precision=EXACT,
                    preferred_element_type=jnp.float32,
                )
                lanes = lax.broadcasted_iota(jnp.int32, (bottom - top, n), 1)
                x[top:bottom, :] = jnp.where((lanes >= r0) & (lanes < r1), 0.0, x[top:bottom, :]) - update


def lower_rows(x, first, last):
    row_at = lax.broadcasted_iota(jnp.int32, (last - first, last), 0) + first
    col_at = lax.broadcasted_iota(jnp.int32, (last - first, last), 1)
    return jnp.where(col_at <= row_at, x[first:last, :last], 0.0)


def times(rhs, inverse):
    return lax.dot_general(
        rhs, inverse, (((1,), (1,)), ((), ())), precision=EXACT, preferred_element_type=jnp.float32
    )


def cost(micros):
    return pl.CostEstimate(flops=int(micros * 1e6), bytes_accessed=int(micros * 1e6), transcendentals=0)


def params(mebibytes):
    return pltpu.CompilerParams(vmem_limit_bytes=mebibytes * 1024 * 1024)


def factor_kernel(diag_ref, panel_ref, inverse_ref, own_ref, x_ref):
    n = diag_ref.shape[0]
    x_ref[...] = diag_ref[...]
    eliminate(x_ref, 0, n)
    inverse = lower_rows(x_ref, 0, n)
    inverse_ref[...] = inverse
    own_ref[...] = times(panel_ref[...], inverse).astype(jnp.bfloat16)


def factor(diag_tile, panel_block):
    return pl.pallas_call(
        factor_kernel,
        out_shape=(
            jax.ShapeDtypeStruct(diag_tile.shape, jnp.float32),
            jax.ShapeDtypeStruct(panel_block.shape, jnp.bfloat16),
        ),
        scratch_shapes=[pltpu.VMEM(diag_tile.shape, jnp.float32)],
        cost_estimate=cost(7),
        compiler_params=params(8),
        name="factor",
    )(*(pltpu.with_memory_space_constraint(v, pltpu.HBM) for v in (diag_tile, panel_block)))


def finish_kernel(inverse_ref, panel_ref, head_ref, rows_ref, rest_ref, panel_out_ref, whitened_ref, rest_out_ref):
    inverse = inverse_ref[...]
    whitened = times(head_ref[...], inverse)
    whitened_ref[...] = whitened
    panel_out_ref[...] = times(panel_ref[...], inverse)
    product = lax.dot_general(
        whitened.astype(jnp.bfloat16), rows_ref[...], (((1,), (1,)), ((), ())), preferred_element_type=jnp.float32
    )
    rest_out_ref[...] = rest_ref[...] - product


def finish(inverse, panel_block, vec_head, rows, vec_rest):
    return pl.pallas_call(
        finish_kernel,
        out_shape=tuple(jax.ShapeDtypeStruct(v.shape, jnp.float32) for v in (panel_block, vec_head, vec_rest)),
        cost_estimate=cost(2),
        compiler_params=params(10),
        name="finish",
    )(inverse, *(pltpu.with_memory_space_constraint(v, pltpu.HBM) for v in (panel_block, vec_head)), rows,
      pltpu.with_memory_space_constraint(vec_rest, pltpu.HBM))


def tile(rows_ref, here, block, old):
    product = lax.dot_general(
        rows_ref[here, :], block, (((1,), (1,)), ((), ())), preferred_element_type=jnp.float32
    )
    return (old.astype(jnp.float32) - product).astype(jnp.bfloat16)


def near_update_kernel(at_ref, rows_ref, mine_ref, other_ref, trailing_ref, out_ref, held_ref, buffer_ref, loaded, stored, fetched):
    chunks = loaded.shape[1]
    height, width = rows_ref.shape[0] // chunks, buffer_ref.shape[2]

    def place(b):
        return pl.ds(pl.multiple_of(at_ref[b] * width, width), width)

    heres = [pl.ds(i * height, height) for i in range(chunks)]
    loads = {
        (b, i): pltpu.make_async_copy(trailing_ref.at[heres[i], place(b)], buffer_ref.at[b, heres[i], :], loaded.at[b, i])
        for b in range(2)
        for i in range(chunks)
    }
    fetches = [
        pltpu.make_async_copy(trailing_ref.at[:, place(2 + b)], held_ref.at[b], fetched.at[b])
        for b in range(held_ref.shape[0])
    ]
    stores = []
    for load in loads.values():
        load.start()
    for fetch in fetches:
        fetch.start()
    for b, cols_ref in enumerate((mine_ref, other_ref)):
        for i in range(chunks):
            loads[b, i].wait()
            buffer_ref[b, heres[i], :] = tile(rows_ref, heres[i], cols_ref[...], buffer_ref[b, heres[i], :])
            stores.append(
                pltpu.make_async_copy(buffer_ref.at[b, heres[i], :], out_ref.at[heres[i], place(b)], stored.at[b, i])
            )
            stores[-1].start()
    for copy in stores + fetches:
        copy.wait()


def near_update(at, rows, mine, other, trailing):
    whole, width, chunks = pl.BlockSpec(memory_space=pltpu.VMEM), mine.shape[0], max(1, rows.shape[0] // 256)
    rest = at.shape[0] - 2
    return pl.pallas_call(
        near_update_kernel,
        in_specs=[pl.BlockSpec(memory_space=pltpu.SMEM), whole, whole, whole, pl.BlockSpec(memory_space=pl.ANY)],
        out_specs=(pl.BlockSpec(memory_space=pl.ANY), whole),
        out_shape=(
            pltpu.HBM(trailing.shape, trailing.dtype),
            pltpu.VMEM((rest, rows.shape[0], width), trailing.dtype),
        ),
        scratch_shapes=[
            pltpu.VMEM((2, rows.shape[0], width), trailing.dtype),
            pltpu.SemaphoreType.DMA((2, chunks)),
            pltpu.SemaphoreType.DMA((2, chunks)),
            pltpu.SemaphoreType.DMA((rest,)),
        ],
        cost_estimate=cost(4),
        compiler_params=params(16),
        name="near_update",
    )(at, rows, mine, other, pltpu.with_memory_space_constraint(trailing, pltpu.HBM))


def far_update_kernel(first, at_ref, rows_ref, cols_ref, held_ref, old_ref, out_ref, buffer_ref, sems):
    blocks, chunks = sems.shape
    height, width = rows_ref.shape[0] // chunks, buffer_ref.shape[2]
    stores = []
    for b in range(blocks):
        place = pl.ds(pl.multiple_of(at_ref[first + b] * width, width), width)
        block = cols_ref[b * width : (b + 1) * width, :]
        for i in range(chunks):
            here = pl.ds(i * height, height)
            buffer_ref[b, here, :] = tile(rows_ref, here, block, held_ref[first + b, here, :])
            stores.append(pltpu.make_async_copy(buffer_ref.at[b, here, :], out_ref.at[here, place], sems.at[b, i]))
            stores[-1].start()
    for store in stores:
        store.wait()


def far_update(first, at, rows, cols, held, out):
    whole, width, chunks = pl.BlockSpec(memory_space=pltpu.VMEM), held.shape[2], max(1, rows.shape[0] // 256)
    blocks = cols.shape[0] // width
    return pl.pallas_call(
        functools.partial(far_update_kernel, first),
        in_specs=[pl.BlockSpec(memory_space=pltpu.SMEM), whole, whole, whole, pl.BlockSpec(memory_space=pl.ANY)],
        out_specs=pl.BlockSpec(memory_space=pl.ANY),
        out_shape=pltpu.HBM(out.shape, out.dtype),
        input_output_aliases={4: 0},
        scratch_shapes=[
            pltpu.VMEM((blocks, rows.shape[0], width), out.dtype),
            pltpu.SemaphoreType.DMA((blocks, chunks)),
        ],
        cost_estimate=cost(1.8 * blocks),
        compiler_params=params(10),
        name="far_update",
    )(at, rows, cols, pltpu.with_memory_space_constraint(held, pltpu.VMEM), out)


def after(value, other):
    return lax.optimization_barrier((value, other))[0]


def flip(value, size, k):
    return lax.ppermute(value, "col", [(c, c ^ k) for c in range(size)])


def swap(value, row_size, col_size):
    moves = [(r * col_size + c, (r ^ 1) * col_size + c) for r in range(row_size) for c in range(col_size)]
    parts = jnp.split(value, 2, axis=0)
    return jnp.concatenate([lax.ppermute(part, ("row", "col"), moves) for part in parts], axis=0)


def spread(mine, row_size, col_size, first_after=(), last_after=()):
    row, col = lax.axis_index("row"), lax.axis_index("col")
    apart = (row // 2) ^ col
    steps = (row_size // 2).bit_length() - 1
    held, have = mine, [[0], [0]]
    for step in range(steps):
        moves, arrived = [], apart < 0
        for i in range(2):
            bit = 1 << ((step + i) % steps)
            for d in have[i]:
                moves += [
                    (((c ^ d) * 2 + i) * col_size + c, ((c ^ d ^ bit) * 2 + i) * col_size + c) for c in range(col_size)
                ]
                arrived = arrived | ((apart == d ^ bit) & (row % 2 == i))
            have[i] = have[i] + [d ^ bit for d in have[i]]
        came = lax.ppermute(held, ("row", "col"), moves)
        if step == 0:
            came = after(came, first_after)
        if step == steps - 1:
            came = after(came, last_after)
        held = jnp.where(arrived, came, held)
    return held


def per_device(row_size, col_size, diag_tile, panel_block, trailing, vec_head, vec_rest):
    row, col = lax.axis_index("row"), lax.axis_index("col")
    odd = (col & 1) == 1
    size = panel_block.shape[0]
    inverse, own = factor(diag_tile, panel_block)
    mate = flip(own, col_size, 1)
    ks = range(2, col_size, 2)
    blocks = {0: own}
    for bit in [1 << i for i in range(1, col_size.bit_length() - 1)][::-1]:
        blocks |= {k ^ bit: flip(v, col_size, bit) for k, v in list(blocks.items())}
    evens = jnp.concatenate([blocks[k] for k in ks], axis=0)
    odds = flip(evens, col_size, 1)

    def paired(a, b):
        count = a.shape[0] // size
        a, b = (v.reshape(count, 1, size, v.shape[1]) for v in (a, b))
        both = jnp.where(odd, jnp.concatenate([b, a], axis=1), jnp.concatenate([a, b], axis=1))
        return both.reshape(2 * count * size, a.shape[3])

    width, count = 2 * size, col_size // 2
    near, far = paired(own, mate), paired(evens, odds)
    rows = jnp.zeros((col_size * size, near.shape[1]), near.dtype)
    for p in range(count):
        pair = near if p == 0 else far[(p - 1) * width : p * width]
        rows = lax.dynamic_update_slice_in_dim(rows, pair, ((col >> 1) ^ p) * width, 0)
    near_cols = spread(near, row_size, col_size)

    def places(offsets):
        values = [((row & 1) ^ half) * (col_size // 2) + ((col >> 1) ^ p) for half in range(2) for p in offsets]
        return jnp.stack(values).astype(jnp.int32)

    far_places = places(range(1, count))
    other_cols = swap(near_cols, row_size, col_size)
    panel, whitened, vec_new = finish(inverse, panel_block, vec_head, rows, vec_rest)
    out, held = near_update(jnp.concatenate([places([0]), far_places]), rows, near_cols, other_cols, trailing)
    far_cols = spread(far, row_size, col_size, vec_new, out)
    out = far_update(0, far_places, rows, far_cols, held, out)
    out = far_update(count - 1, far_places, rows, swap(far_cols, row_size, col_size), held, out)
    return (panel, out, whitened, vec_new)


def solution(mesh):
    row_size, col_size = mesh.shape["row"], mesh.shape["col"]
    in_specs = (P(), P(("row", "col"), None), P("row", "col"), P("col", None), P("col", "row"))
    out_specs = (P(("row", "col"), None), P("row", "col"), P("col", None), P("col", "row"))
    return jax.shard_map(
        functools.partial(per_device, row_size, col_size),
        mesh=mesh,
        in_specs=in_specs,
        out_specs=out_specs,
        check_vma=False,
    )
```

time: 158 us -> 56.1 us (0.36)
  other arithmetic: 54.7 us -> 0.54 us
  waiting for transfers between devices: 40.6 us -> 17.9 us
  blocking collectives: 21.8 us -> 0 us
  Pallas kernels: 0 us -> 21 us
  matrix products: 17.6 us -> 0 us
  starting transfers between devices: 0.04 us -> 15.3 us
  between operations: 15.5 us -> 0.9 us
  local copies, waits for them, and re-layouts: 6.87 us -> 0.18 us
    another operation x11 -> x1, other arithmetic: 53.7 us -> 0.07 us  [places(): return jnp.stack(values).astype(jnp.int32)]
    all_gather x1 -> x0, waiting for transfers between devices: 40.6 us -> none  [per_device(): complete = lax.all_gather(row_panel, 'row', axis=0, tiled=True)]
    all_gather x1 -> x0, blocking collectives: 21.8 us -> none  [per_device(): row_panel = lax.all_gather(panel_half, 'col', axis=0, tiled=True)]
    pallas_call x0 -> x5, Pallas kernels: none -> 21 us  [the longest x1 6.64 us: factor(): pl.pallas_call(factor_kernel, out_shape=(jax.ShapeDtypeStruct(diag_tile.s...]
    ppermute x0 -> x11, waiting for transfers between devices: none -> 17.9 us  [the longest x3 12 us: flip(): return lax.ppermute(value, 'col', [(c, c ^ k) for c in range(size)])]
    ppermute x0 -> x11, starting transfers between devices: none -> 15.3 us  [the longest x4 8.44 us: spread(): came = lax.ppermute(held, ('row', 'col'), moves)]
    dot_general x2 -> x0, matrix products: 13.1 us -> none  [the longest x1 10.8 us: per_device(): lax.dot_general(row_panel, col_panel, (((1,), (1,)), ((), ())), preferred...]
    another operation x8 -> x0, matrix products: 4.47 us -> none  [the longest x6 4 us: right_solve(): lax.linalg.triangular_solve(factor, rhs, left_side=False, lower=True, tra...]
  transfers between devices with their start and end apart: 1 -> 11, of which waited for: 1 -> 5; matrix products, arithmetic and copies ran while one was open for 3% -> 1% of each run, Pallas kernels for 0% -> 22%
where the time goes in v1:
time: 56.1 us; the launch traced here: 55.9 us
  Pallas kernels  21 us (37%)
  waiting for transfers between devices  17.9 us (32%)
  starting transfers between devices  15.3 us (27%)
  between operations  0.9 us (2%)
    ppermute x3, waiting for transfers between devices, flip(): return lax.ppermute(value, 'col', [(c, c ^ k) for c in range(size)])  12 us
    ppermute x4, starting transfers between devices, spread(): came = lax.ppermute(held, ('row', 'col'), moves)  8.44 us
    pallas_call x1, Pallas kernels, factor(): pl.pallas_call(factor_kernel, out_shape=(jax.ShapeDtypeStruct(diag_tile.s...  6.64 us
    pallas_call x1, Pallas kernels, near_update(): pl.pallas_call(near_update_kernel, in_specs=[pl.BlockSpec(memory_space=pl...  6.54 us
    ppermute x3, starting transfers between devices, flip(): return lax.ppermute(value, 'col', [(c, c ^ k) for c in range(size)])  5.75 us
    ppermute x4, waiting for transfers between devices, spread(): came = lax.ppermute(held, ('row', 'col'), moves)  4.8 us
    pallas_call x2, Pallas kernels, far_update(): pl.pallas_call(functools.partial(far_update_kernel, first), in_specs=[pl....  4.64 us
    pallas_call x1, Pallas kernels, finish(): pl.pallas_call(finish_kernel, out_shape=tuple((jax.ShapeDtypeStruct(v.sha...  3.18 us
  transfers between devices with their start and end apart: 11, of which 5 were waited for; matrix products, arithmetic and copies ran while one was open for 1% of the time, Pallas kernels for 22%

profile of v1, /device:TPU:0, one launch (start us, length us, event | category | flops | bytes accessed | tf_op | source)
XLA Modules:
  0.0 55.9 jit_solution(13135939999689088621)
XLA Ops:
  0.6 6.6 %factor.1 = (f32[256,256]{1,0:T(8,128)S(1)}, bf16[384,256]{1,0:T(8,128)(2,1)S(1)}) custom-call(f32[256,256]{1,0:T(8,128)} %diag_ref.1, f32[384,256]{1,0:T(8,128)} %panel_ref.3), custom_call_target="tpu_custom_call" | custom-call | flops 7000000 | bytes 7000000 | tf_op jit(solution)/shard_map/factor/pallas_call | solution.py:130
  7.3 3.1 %collective-permute-start = (bf16[384,256]{1,0:T(8,128)(2,1)S(1)}, bf16[384,256]{1,0:T(8,128)(2,1)S(1)}, u32[]{:S(2)}, u32[]{:S(2)}) collective-permute-start(bf16[384,256]{1,0:T(8,128)(2,1)S(1)} %get-tuple-element.14), channel_id=1, source_target_pairs={{0,1},{1,0},{2,3},{3,2},{4,5},{5,4},{6,7},{7,6},{8,9},{9,8},{10,11... | collective-permute-start | bytes 589832 | tf_op jit(solution)/shard_map/ppermute | solution.py:269
  10.4 2.6 %collective-permute-start.1 = (bf16[384,256]{1,0:T(8,128)(2,1)S(1)}, bf16[384,256]{1,0:T(8,128)(2,1)S(1)}, u32[]{:S(2)}, u32[]{:S(2)}) collective-permute-start(bf16[384,256]{1,0:T(8,128)(2,1)S(1)} %get-tuple-element.14), channel_id=1, source_target_pairs={{0,2},{1,3},{2,0},{3,1},{4,6},{5,7},{6,4},{7,5},{8,10},{9,11},{10,... | collective-permute-start | bytes 589832 | tf_op jit(solution)/shard_map/ppermute | solution.py:269
  13.0 6.4 %collective-permute-done = bf16[384,256]{1,0:T(8,128)(2,1)S(1)} collective-permute-done((bf16[384,256]{1,0:T(8,128)(2,1)S(1)}, bf16[384,256]{1,0:T(8,128)(2,1)S(1)}, u32[]{:S(2)}, u32[]{:S(2)}) %collective-permute-start) | collective-permute-done | bytes 196640 | tf_op jit(solution)/shard_map/ppermute | solution.py:269
  19.4 3.6 %collective-permute-start.5 = (bf16[768,256]{1,0:T(8,128)(2,1)S(1)}, bf16[768,256]{1,0:T(8,128)(2,1)S(1)}, u32[]{:S(2)}, u32[]{:S(2)}) collective-permute-start(bf16[768,256]{1,0:T(8,128)(2,1)S(1)} %bitcast.13), channel_id=1, source_target_pairs={{0,8},{9,1},{18,26},{27,19},{4,20},{13,29},{22,6},{31,15}} | collective-permute-start | bytes 1179656 | tf_op jit(solution)/shard_map/ppermute | solution.py:293
  23.0 0.0 collective-permute-done.1
  23.0 0.1 collective-permute-start.2
  23.2 5.6 %collective-permute-done.2 = bf16[384,256]{1,0:T(8,128)(2,1)S(1)} collective-permute-done((bf16[384,256]{1,0:T(8,128)(2,1)S(1)}, bf16[384,256]{1,0:T(8,128)(2,1)S(1)}, u32[]{:S(2)}, u32[]{:S(2)}) %collective-permute-start.2) | collective-permute-done | bytes 196640 | tf_op jit(solution)/shard_map/ppermute | solution.py:269
  28.8 2.2 %collective-permute-start.3 = (bf16[768,256]{1,0:T(8,128)(2,1)S(1)}, bf16[768,256]{1,0:T(8,128)(2,1)S(1)}, u32[]{:S(2)}, u32[]{:S(2)}) collective-permute-start(bf16[768,256]{1,0:T(8,128)(2,1)S(1)} %bitcast.15), channel_id=1, source_target_pairs={{0,8},{9,1},{18,26},{27,19},{4,20},{13,29},{22,6},{31,15}} | collective-permute-start | bytes 1179656 | tf_op jit(solution)/shard_map/ppermute | solution.py:293
  31.0 0.0 collective-permute-done.5
  31.1 0.1 broadcast_select_fusion
  31.1 1.3 %collective-permute-start.6 = (bf16[768,256]{1,0:T(8,128)(2,1)S(1)}, bf16[768,256]{1,0:T(8,128)(2,1)S(1)}, u32[]{:S(2)}, u32[]{:S(2)}) collective-permute-start(bf16[768,256]{1,0:T(8,128)(2,1)S(1)} %broadcast_select_fusion), channel_id=1, source_target_pairs={{0,16},{9,25},{18,2},{27,11},{8,24},{1,17},{26,10},{19,3},{4,12},{... | collective-permute-start | bytes 1179656 | tf_op jit(solution)/shard_map/ppermute | solution.py:293
  32.5 0.1 broadcast_in_dim.3
  32.6 3.2 %finish.1 = (f32[384,256]{1,0:T(8,128)}, f32[128,256]{1,0:T(8,128)}, f32[128,1536]{1,0:T(8,128)}) custom-call(f32[256,256]{1,0:T(8,128)S(1)} %get-tuple-element.13.inverse_ref, f32[384,256]{1,0:T(8,128)} %panel_ref.3, f32[128,256]{1,0:T(8,128)} %head_ref.1, bf16[1536,256]{1,0:T(8,128)(2,1)S(1)} %constant_dynamic-update-slice_fusion.rows_ref, ...), custom_call_target="tpu_custom_call" | custom-call | flops 2000000 | bytes 2000000 | tf_op jit(solution)/shard_map/finish/pallas_call | solution.py:155
  35.8 4.8 %collective-permute-done.3 = bf16[768,256]{1,0:T(8,128)(2,1)S(1)} collective-permute-done((bf16[768,256]{1,0:T(8,128)(2,1)S(1)}, bf16[768,256]{1,0:T(8,128)(2,1)S(1)}, u32[]{:S(2)}, u32[]{:S(2)}) %collective-permute-start.3) | collective-permute-done | bytes 393248 | tf_op jit(solution)/shard_map/ppermute | solution.py:293
  40.6 0.1 broadcast_select_fusion.1
  40.7 1.3 %collective-permute-start.4 = (bf16[768,256]{1,0:T(8,128)(2,1)S(1)}, bf16[768,256]{1,0:T(8,128)(2,1)S(1)}, u32[]{:S(2)}, u32[]{:S(2)}) collective-permute-start(bf16[768,256]{1,0:T(8,128)(2,1)S(1)} %broadcast_select_fusion.1), channel_id=1, source_target_pairs={{0,16},{9,25},{18,2},{27,11},{8,24},{1,17},{26,10},{19,3},{4,12},{... | collective-permute-start | bytes 1179656 | tf_op jit(solution)/shard_map/ppermute | solution.py:293
  42.0 0.0 collective-permute-done.6
  42.1 0.1 collective-permute-start.7
  42.2 0.5 collective-permute-start.8
  42.6 0.1 pad_add_fusion.1.at_ref
  42.7 0.9 %collective-permute-done.7 = bf16[384,256]{1,0:T(8,128)(2,1)S(1)} collective-permute-done((bf16[384,256]{1,0:T(8,128)(2,1)S(1)}, bf16[384,256]{1,0:T(8,128)(2,1)S(1)}, u32[]{:S(2)}, u32[]{:S(2)}) %collective-permute-start.7) | collective-permute-done | bytes 196640 | tf_op jit(solution)/shard_map/ppermute | solution.py:275
  43.6 0.3 collective-permute-done.8
  43.9 6.5 %near_update.1 = (bf16[1536,3072]{1,0:T(8,128)(2,1)}, bf16[2,1536,768]{2,1,0:T(8,128)(2,1)S(1)}) custom-call(s32[4]{0:T(128)S(1)} %pad_add_fusion.1.at_ref, bf16[1536,256]{1,0:T(8,128)(2,1)S(1)} %constant_dynamic-update-slice_fusion.rows_ref, bf16[768,256]{1,0:T(8,128)(2,1)S(1)} %broadcast_select_fusion.3.mine_ref, ...), custom_call_target="tpu_custom_call" | custom-call | flops 4000000 | bytes 4000000 | tf_op jit(solution)/shard_map/near_update/pallas_call | solution.py:209
  50.4 0.0 collective-permute-done.4
  50.5 0.3 collective-permute-start.9
  50.8 0.3 collective-permute-start.10
  51.1 0.1 pad_add_fusion.at_ref
  51.2 2.3 %far_update.2.old_ref = bf16[1536,3072]{1,0:T(8,128)(2,1)} custom-call(s32[2]{0:T(128)S(1)} %pad_add_fusion.at_ref, bf16[1536,256]{1,0:T(8,128)(2,1)S(1)} %constant_dynamic-update-slice_fusion.rows_ref, bf16[768,256]{1,0:T(8,128)(2,1)S(1)} %broadcast_select_fusion.2.cols_ref, ...), custom_call_target="tpu_custom_call", output_to_operand_aliasing={{}: (4, {})} | custom-call | flops 1800000 | bytes 1800000 | tf_op jit(solution)/shard_map/far_update/pallas_call | solution.py:248
  53.5 0.0 collective-permute-done.9
  53.5 0.0 collective-permute-done.10
  53.6 2.3 %far_update.3 = bf16[1536,3072]{1,0:T(8,128)(2,1)} custom-call(s32[2]{0:T(128)S(1)} %pad_add_fusion.at_ref, bf16[1536,256]{1,0:T(8,128)(2,1)S(1)} %constant_dynamic-update-slice_fusion.rows_ref, bf16[768,256]{1,0:T(8,128)(2,1)S(1)} %pad_maximum_fusion.1.cols_ref, ...), custom_call_target="tpu_custom_call", output_to_operand_aliasing={{}: (4, {})} | custom-call | flops 1800000 | bytes 1800000 | tf_op jit(solution)/shard_map/far_update/pallas_call | solution.py:248
  (10 shorter events, 0.4 us)
Async XLA Ops:
  7.3 12.1 %collective-permute-start = (bf16[384,256]{1,0:T(8,128)(2,1)S(1)}, bf16[384,256]{1,0:T(8,128)(2,1)S(1)}, u32[]{:S(2)}, u32[]{:S(2)}) collective-permute-start(bf16[384,256]{1,0:T(8,128)(2,1)S(1)} %get-tuple-element.14), channel_id=1, source_target_pairs={{0,1},{1,0},{2,3},{3,2},{4,5},{5,4},{6,7},{7,6},{8,9},{9,8},{10,11... | collective-permute-start | bytes 589832 | tf_op jit(solution)/shard_map/ppermute | solution.py:269
  10.4 12.6 %collective-permute-start.1 = (bf16[384,256]{1,0:T(8,128)(2,1)S(1)}, bf16[384,256]{1,0:T(8,128)(2,1)S(1)}, u32[]{:S(2)}, u32[]{:S(2)}) collective-permute-start(bf16[384,256]{1,0:T(8,128)(2,1)S(1)} %get-tuple-element.14), channel_id=1, source_target_pairs={{0,2},{1,3},{2,0},{3,1},{4,6},{5,7},{6,4},{7,5},{8,10},{9,11},{10,... | collective-permute-start | bytes 589832 | tf_op jit(solution)/shard_map/ppermute | solution.py:269
  19.4 11.6 %collective-permute-start.5 = (bf16[768,256]{1,0:T(8,128)(2,1)S(1)}, bf16[768,256]{1,0:T(8,128)(2,1)S(1)}, u32[]{:S(2)}, u32[]{:S(2)}) collective-permute-start(bf16[768,256]{1,0:T(8,128)(2,1)S(1)} %bitcast.13), channel_id=1, source_target_pairs={{0,8},{9,1},{18,26},{27,19},{4,20},{13,29},{22,6},{31,15}} | collective-permute-start | bytes 1179656 | tf_op jit(solution)/shard_map/ppermute | solution.py:293
  23.0 5.7 %collective-permute-start.2 = (bf16[384,256]{1,0:T(8,128)(2,1)S(1)}, bf16[384,256]{1,0:T(8,128)(2,1)S(1)}, u32[]{:S(2)}, u32[]{:S(2)}) collective-permute-start(bf16[384,256]{1,0:T(8,128)(2,1)S(1)} %collective-permute-done.1), channel_id=1, source_target_pairs={{0,1},{1,0},{2,3},{3,2},{4,5},{5,4},{6,7},{7,6},{8,9},{9,8},{10,11... | collective-permute-start | bytes 589832 | tf_op jit(solution)/shard_map/ppermute | solution.py:269
  28.8 11.8 %collective-permute-start.3 = (bf16[768,256]{1,0:T(8,128)(2,1)S(1)}, bf16[768,256]{1,0:T(8,128)(2,1)S(1)}, u32[]{:S(2)}, u32[]{:S(2)}) collective-permute-start(bf16[768,256]{1,0:T(8,128)(2,1)S(1)} %bitcast.15), channel_id=1, source_target_pairs={{0,8},{9,1},{18,26},{27,19},{4,20},{13,29},{22,6},{31,15}} | collective-permute-start | bytes 1179656 | tf_op jit(solution)/shard_map/ppermute | solution.py:293
  31.1 10.8 %collective-permute-start.6 = (bf16[768,256]{1,0:T(8,128)(2,1)S(1)}, bf16[768,256]{1,0:T(8,128)(2,1)S(1)}, u32[]{:S(2)}, u32[]{:S(2)}) collective-permute-start(bf16[768,256]{1,0:T(8,128)(2,1)S(1)} %broadcast_select_fusion), channel_id=1, source_target_pairs={{0,16},{9,25},{18,2},{27,11},{8,24},{1,17},{26,10},{19,3},{4,12},{... | collective-permute-start | bytes 1179656 | tf_op jit(solution)/shard_map/ppermute | solution.py:293
  40.7 9.8 %collective-permute-start.4 = (bf16[768,256]{1,0:T(8,128)(2,1)S(1)}, bf16[768,256]{1,0:T(8,128)(2,1)S(1)}, u32[]{:S(2)}, u32[]{:S(2)}) collective-permute-start(bf16[768,256]{1,0:T(8,128)(2,1)S(1)} %broadcast_select_fusion.1), channel_id=1, source_target_pairs={{0,16},{9,25},{18,2},{27,11},{8,24},{1,17},{26,10},{19,3},{4,12},{... | collective-permute-start | bytes 1179656 | tf_op jit(solution)/shard_map/ppermute | solution.py:293
  42.1 1.5 %collective-permute-start.7 = (bf16[384,256]{1,0:T(8,128)(2,1)S(1)}, bf16[384,256]{1,0:T(8,128)(2,1)S(1)}, u32[]{:S(2)}, u32[]{:S(2)}) collective-permute-start(bf16[384,256]{1,0:T(8,128)(2,1)S(1)} %get-tuple-element.24), channel_id=1, source_target_pairs={{0,4},{1,5},{2,6},{3,7},{4,0},{5,1},{6,2},{7,3},{8,12},{9,13},{10,... | collective-permute-start | bytes 589832 | tf_op jit(solution)/shard_map/ppermute | solution.py:275
  42.2 1.7 %collective-permute-start.8 = (bf16[384,256]{1,0:T(8,128)(2,1)S(1)}, bf16[384,256]{1,0:T(8,128)(2,1)S(1)}, u32[]{:S(2)}, u32[]{:S(2)}) collective-permute-start(bf16[384,256]{1,0:T(8,128)(2,1)S(1)} %get-tuple-element.25), channel_id=1, source_target_pairs={{0,4},{1,5},{2,6},{3,7},{4,0},{5,1},{6,2},{7,3},{8,12},{9,13},{10,... | collective-permute-start | bytes 589832 | tf_op jit(solution)/shard_map/ppermute | solution.py:275
  50.5 3.0 %collective-permute-start.9 = (bf16[384,256]{1,0:T(8,128)(2,1)S(1)}, bf16[384,256]{1,0:T(8,128)(2,1)S(1)}, u32[]{:S(2)}, u32[]{:S(2)}) collective-permute-start(bf16[384,256]{1,0:T(8,128)(2,1)S(1)} %get-tuple-element.22), channel_id=1, source_target_pairs={{0,4},{1,5},{2,6},{3,7},{4,0},{5,1},{6,2},{7,3},{8,12},{9,13},{10,... | collective-permute-start | bytes 589832 | tf_op jit(solution)/shard_map/ppermute | solution.py:275
  50.8 2.7 %collective-permute-start.10 = (bf16[384,256]{1,0:T(8,128)(2,1)S(1)}, bf16[384,256]{1,0:T(8,128)(2,1)S(1)}, u32[]{:S(2)}, u32[]{:S(2)}) collective-permute-start(bf16[384,256]{1,0:T(8,128)(2,1)S(1)} %get-tuple-element.23), channel_id=1, source_target_pairs={{0,4},{1,5},{2,6},{3,7},{4,0},{5,1},{6,2},{7,3},{8,12},{9,13},{10,... | collective-permute-start | bytes 589832 | tf_op jit(solution)/shard_map/ppermute | solution.py:275

commit v2 on v1

--- a/solution.py
+++ b/solution.py
@@ -183,8 +183,10 @@
         for i in range(chunks)
     }
     fetches = [
-        pltpu.make_async_copy(trailing_ref.at[:, place(2 + b)], held_ref.at[b], fetched.at[b])
-        for b in range(held_ref.shape[0])
+        pltpu.make_async_copy(
+            trailing_ref.at[:, place(2 + b)], held_ref.at[:, pl.ds(b * width, width)], fetched.at[b]
+        )
+        for b in range(fetched.shape[0])
     ]
     stores = []
     for load in loads.values():
@@ -204,7 +206,7 @@
 
 
 def near_update(at, rows, mine, other, trailing):
-    whole, width, chunks = pl.BlockSpec(memory_space=pltpu.VMEM), mine.shape[0], max(1, rows.shape[0] // 256)
+    whole, width, chunks = pl.BlockSpec(memory_space=pltpu.VMEM), mine.shape[0], max(1, rows.shape[0] // 512)
     rest = at.shape[0] - 2
     return pl.pallas_call(
         near_update_kernel,
@@ -212,7 +214,7 @@
         out_specs=(pl.BlockSpec(memory_space=pl.ANY), whole),
         out_shape=(
             pltpu.HBM(trailing.shape, trailing.dtype),
-            pltpu.VMEM((rest, rows.shape[0], width), trailing.dtype),
+            pltpu.VMEM((rows.shape[0], rest * width), trailing.dtype),
         ),
         scratch_shapes=[
             pltpu.VMEM((2, rows.shape[0], width), trailing.dtype),
@@ -235,7 +237,7 @@
         block = cols_ref[b * width : (b + 1) * width, :]
         for i in range(chunks):
             here = pl.ds(i * height, height)
-            buffer_ref[b, here, :] = tile(rows_ref, here, block, held_ref[first + b, here, :])
+            buffer_ref[b, here, :] = tile(rows_ref, here, block, held_ref[here, (first + b) * width : (first + b + 1) * width])
             stores.append(pltpu.make_async_copy(buffer_ref.at[b, here, :], out_ref.at[here, place], sems.at[b, i]))
             stores[-1].start()
     for store in stores:
@@ -243,7 +245,8 @@
 
 
 def far_update(first, at, rows, cols, held, out):
-    whole, width, chunks = pl.BlockSpec(memory_space=pltpu.VMEM), held.shape[2], max(1, rows.shape[0] // 256)
+    whole, chunks = pl.BlockSpec(memory_space=pltpu.VMEM), max(1, rows.shape[0] // 256)
+    width = held.shape[1] // (at.shape[0])
     blocks = cols.shape[0] // width
     return pl.pallas_call(
         functools.partial(far_update_kernel, first),

time: 56.1 us -> 55.5 us (0.989)
  Pallas kernels: 21 us -> 20.4 us
    pallas_call x1, Pallas kernels: 6.54 us -> 5.9 us  [near_update(): pl.pallas_call(near_update_kernel, in_specs=[pl.BlockSpec(memory_space=pl...]
  transfers between devices with their start and end apart: 11 -> 11, of which waited for: 5 -> 5; matrix products, arithmetic and copies ran while one was open for 1% -> 1% of each run, Pallas kernels for 22% -> 21%
where the time goes in v2:
time: 55.5 us; the launch traced here: 55.3 us
  Pallas kernels  20.4 us (37%)
  waiting for transfers between devices  17.9 us (32%)
  starting transfers between devices  15.3 us (28%)
  between operations  0.9 us (2%)
    ppermute x3, waiting for transfers between devices, flip(): return lax.ppermute(value, 'col', [(c, c ^ k) for c in range(size)])  12 us
    ppermute x4, starting transfers between devices, spread(): came = lax.ppermute(held, ('row', 'col'), moves)  8.44 us
    pallas_call x1, Pallas kernels, factor(): pl.pallas_call(factor_kernel, out_shape=(jax.ShapeDtypeStruct(diag_tile.s...  6.64 us
    pallas_call x1, Pallas kernels, near_update(): pl.pallas_call(near_update_kernel, in_specs=[pl.BlockSpec(memory_space=pl...  5.9 us
    ppermute x3, starting transfers between devices, flip(): return lax.ppermute(value, 'col', [(c, c ^ k) for c in range(size)])  5.75 us
    ppermute x4, waiting for transfers between devices, spread(): came = lax.ppermute(held, ('row', 'col'), moves)  4.8 us
    pallas_call x2, Pallas kernels, far_update(): pl.pallas_call(functools.partial(far_update_kernel, first), in_specs=[pl....  4.64 us
    pallas_call x1, Pallas kernels, finish(): pl.pallas_call(finish_kernel, out_shape=tuple((jax.ShapeDtypeStruct(v.sha...  3.18 us
  transfers between devices with their start and end apart: 11, of which 5 were waited for; matrix products, arithmetic and copies ran while one was open for 1% of the time, Pallas kernels for 21%

profile of v2, /device:TPU:0, one launch (start us, length us, event | category | flops | bytes accessed | tf_op | source)
XLA Modules:
  0.0 55.3 jit_solution(8945353780930962675)
XLA Ops:
  0.6 6.6 %factor.1 = (f32[256,256]{1,0:T(8,128)S(1)}, bf16[384,256]{1,0:T(8,128)(2,1)S(1)}) custom-call(f32[256,256]{1,0:T(8,128)} %diag_ref.1, f32[384,256]{1,0:T(8,128)} %panel_ref.3), custom_call_target="tpu_custom_call" | custom-call | flops 7000000 | bytes 7000000 | tf_op jit(solution)/shard_map/factor/pallas_call | solution.py:130
  7.3 3.1 %collective-permute-start = (bf16[384,256]{1,0:T(8,128)(2,1)S(1)}, bf16[384,256]{1,0:T(8,128)(2,1)S(1)}, u32[]{:S(2)}, u32[]{:S(2)}) collective-permute-start(bf16[384,256]{1,0:T(8,128)(2,1)S(1)} %get-tuple-element.14), channel_id=1, source_target_pairs={{0,1},{1,0},{2,3},{3,2},{4,5},{5,4},{6,7},{7,6},{8,9},{9,8},{10,11... | collective-permute-start | bytes 589832 | tf_op jit(solution)/shard_map/ppermute | solution.py:272
  10.4 2.6 %collective-permute-start.1 = (bf16[384,256]{1,0:T(8,128)(2,1)S(1)}, bf16[384,256]{1,0:T(8,128)(2,1)S(1)}, u32[]{:S(2)}, u32[]{:S(2)}) collective-permute-start(bf16[384,256]{1,0:T(8,128)(2,1)S(1)} %get-tuple-element.14), channel_id=1, source_target_pairs={{0,2},{1,3},{2,0},{3,1},{4,6},{5,7},{6,4},{7,5},{8,10},{9,11},{10,... | collective-permute-start | bytes 589832 | tf_op jit(solution)/shard_map/ppermute | solution.py:272
  13.0 6.4 %collective-permute-done = bf16[384,256]{1,0:T(8,128)(2,1)S(1)} collective-permute-done((bf16[384,256]{1,0:T(8,128)(2,1)S(1)}, bf16[384,256]{1,0:T(8,128)(2,1)S(1)}, u32[]{:S(2)}, u32[]{:S(2)}) %collective-permute-start) | collective-permute-done | bytes 196640 | tf_op jit(solution)/shard_map/ppermute | solution.py:272
  19.4 3.6 %collective-permute-start.5 = (bf16[768,256]{1,0:T(8,128)(2,1)S(1)}, bf16[768,256]{1,0:T(8,128)(2,1)S(1)}, u32[]{:S(2)}, u32[]{:S(2)}) collective-permute-start(bf16[768,256]{1,0:T(8,128)(2,1)S(1)} %bitcast.13), channel_id=1, source_target_pairs={{0,8},{9,1},{18,26},{27,19},{4,20},{13,29},{22,6},{31,15}} | collective-permute-start | bytes 1179656 | tf_op jit(solution)/shard_map/ppermute | solution.py:296
  23.0 0.0 collective-permute-done.1
  23.0 0.1 collective-permute-start.2
  23.2 5.6 %collective-permute-done.2 = bf16[384,256]{1,0:T(8,128)(2,1)S(1)} collective-permute-done((bf16[384,256]{1,0:T(8,128)(2,1)S(1)}, bf16[384,256]{1,0:T(8,128)(2,1)S(1)}, u32[]{:S(2)}, u32[]{:S(2)}) %collective-permute-start.2) | collective-permute-done | bytes 196640 | tf_op jit(solution)/shard_map/ppermute | solution.py:272
  28.8 2.2 %collective-permute-start.3 = (bf16[768,256]{1,0:T(8,128)(2,1)S(1)}, bf16[768,256]{1,0:T(8,128)(2,1)S(1)}, u32[]{:S(2)}, u32[]{:S(2)}) collective-permute-start(bf16[768,256]{1,0:T(8,128)(2,1)S(1)} %bitcast.15), channel_id=1, source_target_pairs={{0,8},{9,1},{18,26},{27,19},{4,20},{13,29},{22,6},{31,15}} | collective-permute-start | bytes 1179656 | tf_op jit(solution)/shard_map/ppermute | solution.py:296
  31.0 0.0 collective-permute-done.5
  31.1 0.1 broadcast_select_fusion
  31.1 1.3 %collective-permute-start.6 = (bf16[768,256]{1,0:T(8,128)(2,1)S(1)}, bf16[768,256]{1,0:T(8,128)(2,1)S(1)}, u32[]{:S(2)}, u32[]{:S(2)}) collective-permute-start(bf16[768,256]{1,0:T(8,128)(2,1)S(1)} %broadcast_select_fusion), channel_id=1, source_target_pairs={{0,16},{9,25},{18,2},{27,11},{8,24},{1,17},{26,10},{19,3},{4,12},{... | collective-permute-start | bytes 1179656 | tf_op jit(solution)/shard_map/ppermute | solution.py:296
  32.5 0.1 broadcast_in_dim.3
  32.6 3.2 %finish.1 = (f32[384,256]{1,0:T(8,128)}, f32[128,256]{1,0:T(8,128)}, f32[128,1536]{1,0:T(8,128)}) custom-call(f32[256,256]{1,0:T(8,128)S(1)} %get-tuple-element.13.inverse_ref, f32[384,256]{1,0:T(8,128)} %panel_ref.3, f32[128,256]{1,0:T(8,128)} %head_ref.1, bf16[1536,256]{1,0:T(8,128)(2,1)S(1)} %constant_dynamic-update-slice_fusion.rows_ref, ...), custom_call_target="tpu_custom_call" | custom-call | flops 2000000 | bytes 2000000 | tf_op jit(solution)/shard_map/finish/pallas_call | solution.py:155
  35.8 4.8 %collective-permute-done.3 = bf16[768,256]{1,0:T(8,128)(2,1)S(1)} collective-permute-done((bf16[768,256]{1,0:T(8,128)(2,1)S(1)}, bf16[768,256]{1,0:T(8,128)(2,1)S(1)}, u32[]{:S(2)}, u32[]{:S(2)}) %collective-permute-start.3) | collective-permute-done | bytes 393248 | tf_op jit(solution)/shard_map/ppermute | solution.py:296
  40.6 0.1 broadcast_select_fusion.1
  40.7 1.3 %collective-permute-start.4 = (bf16[768,256]{1,0:T(8,128)(2,1)S(1)}, bf16[768,256]{1,0:T(8,128)(2,1)S(1)}, u32[]{:S(2)}, u32[]{:S(2)}) collective-permute-start(bf16[768,256]{1,0:T(8,128)(2,1)S(1)} %broadcast_select_fusion.1), channel_id=1, source_target_pairs={{0,16},{9,25},{18,2},{27,11},{8,24},{1,17},{26,10},{19,3},{4,12},{... | collective-permute-start | bytes 1179656 | tf_op jit(solution)/shard_map/ppermute | solution.py:296
  42.0 0.0 collective-permute-done.6
  42.1 0.1 collective-permute-start.7
  42.2 0.5 collective-permute-start.8
  42.6 0.1 pad_add_fusion.1.at_ref
  42.7 0.9 %collective-permute-done.7 = bf16[384,256]{1,0:T(8,128)(2,1)S(1)} collective-permute-done((bf16[384,256]{1,0:T(8,128)(2,1)S(1)}, bf16[384,256]{1,0:T(8,128)(2,1)S(1)}, u32[]{:S(2)}, u32[]{:S(2)}) %collective-permute-start.7) | collective-permute-done | bytes 196640 | tf_op jit(solution)/shard_map/ppermute | solution.py:278
  43.6 0.3 collective-permute-done.8
  43.9 5.9 %near_update.1 = (bf16[1536,3072]{1,0:T(8,128)(2,1)}, bf16[1536,1536]{1,0:T(8,128)(2,1)S(1)}) custom-call(s32[4]{0:T(128)S(1)} %pad_add_fusion.1.at_ref, bf16[1536,256]{1,0:T(8,128)(2,1)S(1)} %constant_dynamic-update-slice_fusion.rows_ref, bf16[768,256]{1,0:T(8,128)(2,1)S(1)} %broadcast_select_fusion.3.mine_ref, ...), custom_call_target="tpu_custom_call" | custom-call | flops 4000000 | bytes 4000000 | tf_op jit(solution)/shard_map/near_update/pallas_call | solution.py:211
  49.8 0.0 collective-permute-done.4
  49.9 0.3 collective-permute-start.9
  50.2 0.3 collective-permute-start.10
  50.5 0.1 pad_add_fusion.at_ref
  50.6 2.3 %far_update.2.old_ref = bf16[1536,3072]{1,0:T(8,128)(2,1)} custom-call(s32[2]{0:T(128)S(1)} %pad_add_fusion.at_ref, bf16[1536,256]{1,0:T(8,128)(2,1)S(1)} %constant_dynamic-update-slice_fusion.rows_ref, bf16[768,256]{1,0:T(8,128)(2,1)S(1)} %broadcast_select_fusion.2.cols_ref, ...), custom_call_target="tpu_custom_call", output_to_operand_aliasing={{}: (4, {})} | custom-call | flops 1800000 | bytes 1800000 | tf_op jit(solution)/shard_map/far_update/pallas_call | solution.py:251
  52.9 0.0 collective-permute-done.9
  52.9 0.0 collective-permute-done.10
  52.9 2.3 %far_update.3 = bf16[1536,3072]{1,0:T(8,128)(2,1)} custom-call(s32[2]{0:T(128)S(1)} %pad_add_fusion.at_ref, bf16[1536,256]{1,0:T(8,128)(2,1)S(1)} %constant_dynamic-update-slice_fusion.rows_ref, bf16[768,256]{1,0:T(8,128)(2,1)S(1)} %pad_maximum_fusion.1.cols_ref, bf16[1536,1536]{1,0:T(8,128)(2,1)S(1)} %get-tuple-element.20.held_ref, ...), custom_call_target="tpu_custom_call", output_to_operand_aliasing={{}: (4, {})} | custom-call | flops 1800000 | bytes 1800000 | tf_op jit(solution)/shard_map/far_update/pallas_call | solution.py:251
  (10 shorter events, 0.4 us)
Async XLA Ops:
  7.3 12.1 %collective-permute-start = (bf16[384,256]{1,0:T(8,128)(2,1)S(1)}, bf16[384,256]{1,0:T(8,128)(2,1)S(1)}, u32[]{:S(2)}, u32[]{:S(2)}) collective-permute-start(bf16[384,256]{1,0:T(8,128)(2,1)S(1)} %get-tuple-element.14), channel_id=1, source_target_pairs={{0,1},{1,0},{2,3},{3,2},{4,5},{5,4},{6,7},{7,6},{8,9},{9,8},{10,11... | collective-permute-start | bytes 589832 | tf_op jit(solution)/shard_map/ppermute | solution.py:272
  10.4 12.6 %collective-permute-start.1 = (bf16[384,256]{1,0:T(8,128)(2,1)S(1)}, bf16[384,256]{1,0:T(8,128)(2,1)S(1)}, u32[]{:S(2)}, u32[]{:S(2)}) collective-permute-start(bf16[384,256]{1,0:T(8,128)(2,1)S(1)} %get-tuple-element.14), channel_id=1, source_target_pairs={{0,2},{1,3},{2,0},{3,1},{4,6},{5,7},{6,4},{7,5},{8,10},{9,11},{10,... | collective-permute-start | bytes 589832 | tf_op jit(solution)/shard_map/ppermute | solution.py:272
  19.4 11.6 %collective-permute-start.5 = (bf16[768,256]{1,0:T(8,128)(2,1)S(1)}, bf16[768,256]{1,0:T(8,128)(2,1)S(1)}, u32[]{:S(2)}, u32[]{:S(2)}) collective-permute-start(bf16[768,256]{1,0:T(8,128)(2,1)S(1)} %bitcast.13), channel_id=1, source_target_pairs={{0,8},{9,1},{18,26},{27,19},{4,20},{13,29},{22,6},{31,15}} | collective-permute-start | bytes 1179656 | tf_op jit(solution)/shard_map/ppermute | solution.py:296
  23.0 5.7 %collective-permute-start.2 = (bf16[384,256]{1,0:T(8,128)(2,1)S(1)}, bf16[384,256]{1,0:T(8,128)(2,1)S(1)}, u32[]{:S(2)}, u32[]{:S(2)}) collective-permute-start(bf16[384,256]{1,0:T(8,128)(2,1)S(1)} %collective-permute-done.1), channel_id=1, source_target_pairs={{0,1},{1,0},{2,3},{3,2},{4,5},{5,4},{6,7},{7,6},{8,9},{9,8},{10,11... | collective-permute-start | bytes 589832 | tf_op jit(solution)/shard_map/ppermute | solution.py:272
  28.8 11.8 %collective-permute-start.3 = (bf16[768,256]{1,0:T(8,128)(2,1)S(1)}, bf16[768,256]{1,0:T(8,128)(2,1)S(1)}, u32[]{:S(2)}, u32[]{:S(2)}) collective-permute-start(bf16[768,256]{1,0:T(8,128)(2,1)S(1)} %bitcast.15), channel_id=1, source_target_pairs={{0,8},{9,1},{18,26},{27,19},{4,20},{13,29},{22,6},{31,15}} | collective-permute-start | bytes 1179656 | tf_op jit(solution)/shard_map/ppermute | solution.py:296
  31.1 10.8 %collective-permute-start.6 = (bf16[768,256]{1,0:T(8,128)(2,1)S(1)}, bf16[768,256]{1,0:T(8,128)(2,1)S(1)}, u32[]{:S(2)}, u32[]{:S(2)}) collective-permute-start(bf16[768,256]{1,0:T(8,128)(2,1)S(1)} %broadcast_select_fusion), channel_id=1, source_target_pairs={{0,16},{9,25},{18,2},{27,11},{8,24},{1,17},{26,10},{19,3},{4,12},{... | collective-permute-start | bytes 1179656 | tf_op jit(solution)/shard_map/ppermute | solution.py:296
  40.7 9.2 %collective-permute-start.4 = (bf16[768,256]{1,0:T(8,128)(2,1)S(1)}, bf16[768,256]{1,0:T(8,128)(2,1)S(1)}, u32[]{:S(2)}, u32[]{:S(2)}) collective-permute-start(bf16[768,256]{1,0:T(8,128)(2,1)S(1)} %broadcast_select_fusion.1), channel_id=1, source_target_pairs={{0,16},{9,25},{18,2},{27,11},{8,24},{1,17},{26,10},{19,3},{4,12},{... | collective-permute-start | bytes 1179656 | tf_op jit(solution)/shard_map/ppermute | solution.py:296
  42.1 1.5 %collective-permute-start.7 = (bf16[384,256]{1,0:T(8,128)(2,1)S(1)}, bf16[384,256]{1,0:T(8,128)(2,1)S(1)}, u32[]{:S(2)}, u32[]{:S(2)}) collective-permute-start(bf16[384,256]{1,0:T(8,128)(2,1)S(1)} %get-tuple-element.24), channel_id=1, source_target_pairs={{0,4},{1,5},{2,6},{3,7},{4,0},{5,1},{6,2},{7,3},{8,12},{9,13},{10,... | collective-permute-start | bytes 589832 | tf_op jit(solution)/shard_map/ppermute | solution.py:278
  42.2 1.7 %collective-permute-start.8 = (bf16[384,256]{1,0:T(8,128)(2,1)S(1)}, bf16[384,256]{1,0:T(8,128)(2,1)S(1)}, u32[]{:S(2)}, u32[]{:S(2)}) collective-permute-start(bf16[384,256]{1,0:T(8,128)(2,1)S(1)} %get-tuple-element.25), channel_id=1, source_target_pairs={{0,4},{1,5},{2,6},{3,7},{4,0},{5,1},{6,2},{7,3},{8,12},{9,13},{10,... | collective-permute-start | bytes 589832 | tf_op jit(solution)/shard_map/ppermute | solution.py:278
  49.9 3.0 %collective-permute-start.9 = (bf16[384,256]{1,0:T(8,128)(2,1)S(1)}, bf16[384,256]{1,0:T(8,128)(2,1)S(1)}, u32[]{:S(2)}, u32[]{:S(2)}) collective-permute-start(bf16[384,256]{1,0:T(8,128)(2,1)S(1)} %get-tuple-element.22), channel_id=1, source_target_pairs={{0,4},{1,5},{2,6},{3,7},{4,0},{5,1},{6,2},{7,3},{8,12},{9,13},{10,... | collective-permute-start | bytes 589832 | tf_op jit(solution)/shard_map/ppermute | solution.py:278
  50.2 2.7 %collective-permute-start.10 = (bf16[384,256]{1,0:T(8,128)(2,1)S(1)}, bf16[384,256]{1,0:T(8,128)(2,1)S(1)}, u32[]{:S(2)}, u32[]{:S(2)}) collective-permute-start(bf16[384,256]{1,0:T(8,128)(2,1)S(1)} %get-tuple-element.23), channel_id=1, source_target_pairs={{0,4},{1,5},{2,6},{3,7},{4,0},{5,1},{6,2},{7,3},{8,12},{9,13},{10,... | collective-permute-start | bytes 589832 | tf_op jit(solution)/shard_map/ppermute | solution.py:278

commit v3 on v2

--- a/solution.py
+++ b/solution.py
@@ -274,7 +274,7 @@
 
 def swap(value, row_size, col_size):
     moves = [(r * col_size + c, (r ^ 1) * col_size + c) for r in range(row_size) for c in range(col_size)]
-    parts = jnp.split(value, 2, axis=0)
+    parts = [value]
     return jnp.concatenate([lax.ppermute(part, ("row", "col"), moves) for part in parts], axis=0)
 
 

time: 55.5 us -> 53.5 us (0.964)
  waiting for transfers between devices: 17.9 us -> 13.9 us
  starting transfers between devices: 15.3 us -> 17.4 us
    ppermute x4, starting transfers between devices: 8.44 us -> 11.5 us  [spread(): came = lax.ppermute(held, ('row', 'col'), moves)]
    ppermute x4, waiting for transfers between devices: 4.8 us -> 1.89 us  [spread(): came = lax.ppermute(held, ('row', 'col'), moves)]
    ppermute x4 -> x2, waiting for transfers between devices: 1.14 us -> 0.01 us  [swap(): lax.ppermute(part, ('row', 'col'), moves)]
    ppermute x4 -> x2, starting transfers between devices: 1.14 us -> 0.14 us  [swap(): lax.ppermute(part, ('row', 'col'), moves)]
  transfers between devices with their start and end apart: 11 -> 9, of which waited for: 5 -> 4; matrix products, arithmetic and copies ran while one was open for 1% -> 1% of each run, Pallas kernels for 21% -> 21%
where the time goes in v3:
time: 53.5 us; the launch traced here: 53.2 us
  Pallas kernels  20.4 us (38%)
  starting transfers between devices  17.4 us (33%)
  waiting for transfers between devices  13.9 us (26%)
  between operations  0.9 us (2%)
    ppermute x3, waiting for transfers between devices, flip(): return lax.ppermute(value, 'col', [(c, c ^ k) for c in range(size)])  12 us
    ppermute x4, starting transfers between devices, spread(): came = lax.ppermute(held, ('row', 'col'), moves)  11.5 us
    pallas_call x1, Pallas kernels, factor(): pl.pallas_call(factor_kernel, out_shape=(jax.ShapeDtypeStruct(diag_tile.s...  6.64 us
    pallas_call x1, Pallas kernels, near_update(): pl.pallas_call(near_update_kernel, in_specs=[pl.BlockSpec(memory_space=pl...  5.9 us
    ppermute x3, starting transfers between devices, flip(): return lax.ppermute(value, 'col', [(c, c ^ k) for c in range(size)])  5.75 us
    pallas_call x2, Pallas kernels, far_update(): pl.pallas_call(functools.partial(far_update_kernel, first), in_specs=[pl....  4.64 us
    pallas_call x1, Pallas kernels, finish(): pl.pallas_call(finish_kernel, out_shape=tuple((jax.ShapeDtypeStruct(v.sha...  3.18 us
    ppermute x4, waiting for transfers between devices, spread(): came = lax.ppermute(held, ('row', 'col'), moves)  1.89 us
  transfers between devices with their start and end apart: 9, of which 4 were waited for; matrix products, arithmetic and copies ran while one was open for 1% of the time, Pallas kernels for 21%

profile of v3, /device:TPU:0, one launch (start us, length us, event | category | flops | bytes accessed | tf_op | source)
XLA Modules:
  0.0 53.2 jit_solution(17534672522847242707)
XLA Ops:
  0.6 6.6 %factor.1 = (f32[256,256]{1,0:T(8,128)S(1)}, bf16[384,256]{1,0:T(8,128)(2,1)S(1)}) custom-call(f32[256,256]{1,0:T(8,128)} %diag_ref.1, f32[384,256]{1,0:T(8,128)} %panel_ref.3), custom_call_target="tpu_custom_call" | custom-call | flops 7000000 | bytes 7000000 | tf_op jit(solution)/shard_map/factor/pallas_call | solution.py:130
  7.3 3.1 %collective-permute-start = (bf16[384,256]{1,0:T(8,128)(2,1)S(1)}, bf16[384,256]{1,0:T(8,128)(2,1)S(1)}, u32[]{:S(2)}, u32[]{:S(2)}) collective-permute-start(bf16[384,256]{1,0:T(8,128)(2,1)S(1)} %get-tuple-element.14), channel_id=1, source_target_pairs={{0,1},{1,0},{2,3},{3,2},{4,5},{5,4},{6,7},{7,6},{8,9},{9,8},{10,11... | collective-permute-start | bytes 589832 | tf_op jit(solution)/shard_map/ppermute | solution.py:272
  10.4 2.6 %collective-permute-start.1 = (bf16[384,256]{1,0:T(8,128)(2,1)S(1)}, bf16[384,256]{1,0:T(8,128)(2,1)S(1)}, u32[]{:S(2)}, u32[]{:S(2)}) collective-permute-start(bf16[384,256]{1,0:T(8,128)(2,1)S(1)} %get-tuple-element.14), channel_id=1, source_target_pairs={{0,2},{1,3},{2,0},{3,1},{4,6},{5,7},{6,4},{7,5},{8,10},{9,11},{10,... | collective-permute-start | bytes 589832 | tf_op jit(solution)/shard_map/ppermute | solution.py:272
  13.0 6.4 %collective-permute-done = bf16[384,256]{1,0:T(8,128)(2,1)S(1)} collective-permute-done((bf16[384,256]{1,0:T(8,128)(2,1)S(1)}, bf16[384,256]{1,0:T(8,128)(2,1)S(1)}, u32[]{:S(2)}, u32[]{:S(2)}) %collective-permute-start) | collective-permute-done | bytes 196640 | tf_op jit(solution)/shard_map/ppermute | solution.py:272
  19.4 3.6 %collective-permute-start.5 = (bf16[768,256]{1,0:T(8,128)(2,1)S(1)}, bf16[768,256]{1,0:T(8,128)(2,1)S(1)}, u32[]{:S(2)}, u32[]{:S(2)}) collective-permute-start(bf16[768,256]{1,0:T(8,128)(2,1)S(1)} %bitcast.13), channel_id=1, source_target_pairs={{0,8},{9,1},{18,26},{27,19},{4,20},{13,29},{22,6},{31,15}} | collective-permute-start | bytes 1179656 | tf_op jit(solution)/shard_map/ppermute | solution.py:296
  23.0 0.0 collective-permute-done.1
  23.0 0.1 collective-permute-start.2
  23.1 5.6 %collective-permute-done.2 = bf16[384,256]{1,0:T(8,128)(2,1)S(1)} collective-permute-done((bf16[384,256]{1,0:T(8,128)(2,1)S(1)}, bf16[384,256]{1,0:T(8,128)(2,1)S(1)}, u32[]{:S(2)}, u32[]{:S(2)}) %collective-permute-start.2) | collective-permute-done | bytes 196640 | tf_op jit(solution)/shard_map/ppermute | solution.py:272
  28.8 2.2 %collective-permute-start.3 = (bf16[768,256]{1,0:T(8,128)(2,1)S(1)}, bf16[768,256]{1,0:T(8,128)(2,1)S(1)}, u32[]{:S(2)}, u32[]{:S(2)}) collective-permute-start(bf16[768,256]{1,0:T(8,128)(2,1)S(1)} %bitcast.15), channel_id=1, source_target_pairs={{0,8},{9,1},{18,26},{27,19},{4,20},{13,29},{22,6},{31,15}} | collective-permute-start | bytes 1179656 | tf_op jit(solution)/shard_map/ppermute | solution.py:296
  31.0 0.0 collective-permute-done.5
  31.1 0.1 broadcast_select_fusion
  31.1 1.3 %collective-permute-start.6 = (bf16[768,256]{1,0:T(8,128)(2,1)S(1)}, bf16[768,256]{1,0:T(8,128)(2,1)S(1)}, u32[]{:S(2)}, u32[]{:S(2)}) collective-permute-start(bf16[768,256]{1,0:T(8,128)(2,1)S(1)} %broadcast_select_fusion), channel_id=1, source_target_pairs={{0,16},{9,25},{18,2},{27,11},{8,24},{1,17},{26,10},{19,3},{4,12},{... | collective-permute-start | bytes 1179656 | tf_op jit(solution)/shard_map/ppermute | solution.py:296
  32.5 0.1 broadcast_in_dim.3
  32.6 3.2 %finish.1 = (f32[384,256]{1,0:T(8,128)}, f32[128,256]{1,0:T(8,128)}, f32[128,1536]{1,0:T(8,128)}) custom-call(f32[256,256]{1,0:T(8,128)S(1)} %get-tuple-element.13.inverse_ref, f32[384,256]{1,0:T(8,128)} %panel_ref.3, f32[128,256]{1,0:T(8,128)} %head_ref.1, bf16[1536,256]{1,0:T(8,128)(2,1)S(1)} %constant_dynamic-update-slice_fusion.rows_ref, ...), custom_call_target="tpu_custom_call" | custom-call | flops 2000000 | bytes 2000000 | tf_op jit(solution)/shard_map/finish/pallas_call | solution.py:155
  35.8 1.6 %collective-permute-done.3 = bf16[768,256]{1,0:T(8,128)(2,1)S(1)} collective-permute-done((bf16[768,256]{1,0:T(8,128)(2,1)S(1)}, bf16[768,256]{1,0:T(8,128)(2,1)S(1)}, u32[]{:S(2)}, u32[]{:S(2)}) %collective-permute-start.3) | collective-permute-done | bytes 393248 | tf_op jit(solution)/shard_map/ppermute | solution.py:296
  37.4 0.3 collective-permute-done.6
  37.8 0.1 collective-permute-start.7
  37.8 0.1 broadcast_select_fusion.1
  37.9 4.4 %collective-permute-start.4 = (bf16[768,256]{1,0:T(8,128)(2,1)S(1)}, bf16[768,256]{1,0:T(8,128)(2,1)S(1)}, u32[]{:S(2)}, u32[]{:S(2)}) collective-permute-start(bf16[768,256]{1,0:T(8,128)(2,1)S(1)} %broadcast_select_fusion.1), channel_id=1, source_target_pairs={{0,16},{9,25},{18,2},{27,11},{8,24},{1,17},{26,10},{19,3},{4,12},{... | collective-permute-start | bytes 1179656 | tf_op jit(solution)/shard_map/ppermute | solution.py:296
  42.3 0.1 pad_add_fusion.1.at_ref
  42.4 0.0 collective-permute-done.7.other_ref
  42.4 5.9 %near_update.1 = (bf16[1536,3072]{1,0:T(8,128)(2,1)}, bf16[1536,1536]{1,0:T(8,128)(2,1)S(1)}) custom-call(s32[4]{0:T(128)S(1)} %pad_add_fusion.1.at_ref, bf16[1536,256]{1,0:T(8,128)(2,1)S(1)} %constant_dynamic-update-slice_fusion.rows_ref, bf16[768,256]{1,0:T(8,128)(2,1)S(1)} %broadcast_select_fusion.3.mine_ref, ...), custom_call_target="tpu_custom_call" | custom-call | flops 4000000 | bytes 4000000 | tf_op jit(solution)/shard_map/near_update/pallas_call | solution.py:211
  48.3 0.0 collective-permute-done.4
  48.4 0.1 collective-permute-start.8
  48.5 0.1 pad_add_fusion.at_ref
  48.6 2.3 %far_update.2.old_ref = bf16[1536,3072]{1,0:T(8,128)(2,1)} custom-call(s32[2]{0:T(128)S(1)} %pad_add_fusion.at_ref, bf16[1536,256]{1,0:T(8,128)(2,1)S(1)} %constant_dynamic-update-slice_fusion.rows_ref, bf16[768,256]{1,0:T(8,128)(2,1)S(1)} %broadcast_select_fusion.2.cols_ref, ...), custom_call_target="tpu_custom_call", output_to_operand_aliasing={{}: (4, {})} | custom-call | flops 1800000 | bytes 1800000 | tf_op jit(solution)/shard_map/far_update/pallas_call | solution.py:251
  50.9 0.0 collective-permute-done.8.cols_ref
  50.9 2.3 %far_update.3 = bf16[1536,3072]{1,0:T(8,128)(2,1)} custom-call(s32[2]{0:T(128)S(1)} %pad_add_fusion.at_ref, bf16[1536,256]{1,0:T(8,128)(2,1)S(1)} %constant_dynamic-update-slice_fusion.rows_ref, bf16[768,256]{1,0:T(8,128)(2,1)S(1)} %collective-permute-done.8.cols_ref, ...), custom_call_target="tpu_custom_call", output_to_operand_aliasing={{}: (4, {})} | custom-call | flops 1800000 | bytes 1800000 | tf_op jit(solution)/shard_map/far_update/pallas_call | solution.py:251
  (6 shorter events, 0.3 us)
Async XLA Ops:
  7.3 12.1 %collective-permute-start = (bf16[384,256]{1,0:T(8,128)(2,1)S(1)}, bf16[384,256]{1,0:T(8,128)(2,1)S(1)}, u32[]{:S(2)}, u32[]{:S(2)}) collective-permute-start(bf16[384,256]{1,0:T(8,128)(2,1)S(1)} %get-tuple-element.14), channel_id=1, source_target_pairs={{0,1},{1,0},{2,3},{3,2},{4,5},{5,4},{6,7},{7,6},{8,9},{9,8},{10,11... | collective-permute-start | bytes 589832 | tf_op jit(solution)/shard_map/ppermute | solution.py:272
  10.4 12.6 %collective-permute-start.1 = (bf16[384,256]{1,0:T(8,128)(2,1)S(1)}, bf16[384,256]{1,0:T(8,128)(2,1)S(1)}, u32[]{:S(2)}, u32[]{:S(2)}) collective-permute-start(bf16[384,256]{1,0:T(8,128)(2,1)S(1)} %get-tuple-element.14), channel_id=1, source_target_pairs={{0,2},{1,3},{2,0},{3,1},{4,6},{5,7},{6,4},{7,5},{8,10},{9,11},{10,... | collective-permute-start | bytes 589832 | tf_op jit(solution)/shard_map/ppermute | solution.py:272
  19.4 11.6 %collective-permute-start.5 = (bf16[768,256]{1,0:T(8,128)(2,1)S(1)}, bf16[768,256]{1,0:T(8,128)(2,1)S(1)}, u32[]{:S(2)}, u32[]{:S(2)}) collective-permute-start(bf16[768,256]{1,0:T(8,128)(2,1)S(1)} %bitcast.13), channel_id=1, source_target_pairs={{0,8},{9,1},{18,26},{27,19},{4,20},{13,29},{22,6},{31,15}} | collective-permute-start | bytes 1179656 | tf_op jit(solution)/shard_map/ppermute | solution.py:296
  23.0 5.7 %collective-permute-start.2 = (bf16[384,256]{1,0:T(8,128)(2,1)S(1)}, bf16[384,256]{1,0:T(8,128)(2,1)S(1)}, u32[]{:S(2)}, u32[]{:S(2)}) collective-permute-start(bf16[384,256]{1,0:T(8,128)(2,1)S(1)} %collective-permute-done.1), channel_id=1, source_target_pairs={{0,1},{1,0},{2,3},{3,2},{4,5},{5,4},{6,7},{7,6},{8,9},{9,8},{10,11... | collective-permute-start | bytes 589832 | tf_op jit(solution)/shard_map/ppermute | solution.py:272
  28.8 8.6 %collective-permute-start.3 = (bf16[768,256]{1,0:T(8,128)(2,1)S(1)}, bf16[768,256]{1,0:T(8,128)(2,1)S(1)}, u32[]{:S(2)}, u32[]{:S(2)}) collective-permute-start(bf16[768,256]{1,0:T(8,128)(2,1)S(1)} %bitcast.15), channel_id=1, source_target_pairs={{0,8},{9,1},{18,26},{27,19},{4,20},{13,29},{22,6},{31,15}} | collective-permute-start | bytes 1179656 | tf_op jit(solution)/shard_map/ppermute | solution.py:296
  31.1 6.6 %collective-permute-start.6 = (bf16[768,256]{1,0:T(8,128)(2,1)S(1)}, bf16[768,256]{1,0:T(8,128)(2,1)S(1)}, u32[]{:S(2)}, u32[]{:S(2)}) collective-permute-start(bf16[768,256]{1,0:T(8,128)(2,1)S(1)} %broadcast_select_fusion), channel_id=1, source_target_pairs={{0,16},{9,25},{18,2},{27,11},{8,24},{1,17},{26,10},{19,3},{4,12},{... | collective-permute-start | bytes 1179656 | tf_op jit(solution)/shard_map/ppermute | solution.py:296
  37.8 4.7 %collective-permute-start.7 = (bf16[768,256]{1,0:T(8,128)(2,1)S(1)}, bf16[768,256]{1,0:T(8,128)(2,1)S(1)}, u32[]{:S(2)}, u32[]{:S(2)}) collective-permute-start(bf16[768,256]{1,0:T(8,128)(2,1)S(1)} %broadcast_select_fusion.3.mine_ref), channel_id=1, source_target_pairs={{0,4},{1,5},{2,6},{3,7},{4,0},{5,1},{6,2},{7,3},{8,12},{9,13},{10,... | collective-permute-start | bytes 1179656 | tf_op jit(solution)/shard_map/ppermute | solution.py:278
  37.9 10.4 %collective-permute-start.4 = (bf16[768,256]{1,0:T(8,128)(2,1)S(1)}, bf16[768,256]{1,0:T(8,128)(2,1)S(1)}, u32[]{:S(2)}, u32[]{:S(2)}) collective-permute-start(bf16[768,256]{1,0:T(8,128)(2,1)S(1)} %broadcast_select_fusion.1), channel_id=1, source_target_pairs={{0,16},{9,25},{18,2},{27,11},{8,24},{1,17},{26,10},{19,3},{4,12},{... | collective-permute-start | bytes 1179656 | tf_op jit(solution)/shard_map/ppermute | solution.py:296
  48.4 2.5 %collective-permute-start.8 = (bf16[768,256]{1,0:T(8,128)(2,1)S(1)}, bf16[768,256]{1,0:T(8,128)(2,1)S(1)}, u32[]{:S(2)}, u32[]{:S(2)}) collective-permute-start(bf16[768,256]{1,0:T(8,128)(2,1)S(1)} %broadcast_select_fusion.2.cols_ref), channel_id=1, source_target_pairs={{0,4},{1,5},{2,6},{3,7},{4,0},{5,1},{6,2},{7,3},{8,12},{9,13},{10,... | collective-permute-start | bytes 1179656 | tf_op jit(solution)/shard_map/ppermute | solution.py:278
